TPU v7x, 32 devices: a whole 2x2x4 slice. The times are simulated.
32 devices in a mesh: grp: 2 (over x), seq: 8 (over z, core), dp: 2 (over y).
Axes of the slice: x: 2, y: 2, z: 4, core: 2. Of those that a mesh axis runs over, the one named last changes fastest.
Arguments:
- counts: int32 [2, 8, 2, 256, 1024], P('dp', 'seq', 'grp'), may hold values from 0 to 23
- valid_frames: int32 [2, 1], replicated, may hold values from 2 to 16, as said below
- cotangent: bfloat16 [2, 16, 256, 1024], P('dp', 'seq'), may hold values from -0.125 to 0.125
- pillar_proj: bfloat16 [1024, 1024], replicated, may hold values from -0.1875 to 0.1875
- pillar_gain: float32 [1024], replicated, may hold values from 0.1 to 1.9
- latent_proj: bfloat16 [1024, 1024], replicated, may hold values from -0.1875 to 0.1875
- input_proj: bfloat16 [1024, 1024], replicated, may hold values from -0.1875 to 0.1875
- space_gain: float32 [1024], replicated, may hold values from 0.1 to 1.9
- space_project: bfloat16 [1024, 3072], replicated, may hold values from -0.1875 to 0.1875
- space_output: bfloat16 [1024, 1024], replicated, may hold values from -0.1875 to 0.1875
- time_gain: float32 [1024], replicated, may hold values from 0.1 to 1.9
- time_project: bfloat16 [1024, 3072], replicated, may hold values from -0.1875 to 0.1875
- time_output: bfloat16 [1024, 1024], replicated, may hold values from -0.75 to 0.75
Outputs:
- pillar_grad: float32 [1024, 1024], P(('grp', 'seq', 'dp'))
- latent_grad: float32 [1024, 1024], P(('grp', 'seq', 'dp'))
Inputs may be any that keep to these rules, and one draw needn't show every extreme that they name: `valid_frames`: exactly one scene has all 16 frames valid.
All inputs are finite; a program needn't handle non-finite values.
Results may differ from a plain program's by a relative error of at most 0.0095.
Values may be sent and summed in bfloat16 or wider, within the bound.
A program may use at most 128 MiB of HBM per device.

v0:
```python
import functools

import jax
import jax.numpy as jnp
from jax import lax
from jax.experimental import pallas as pl
from jax.experimental.pallas import tpu as pltpu
from jax.sharding import PartitionSpec as P

CHUNKS = 2
HEADS = 8
FRAMES = 16
ROWS = 32
TILE = 256
GELU = (2.0 / 3.141592653589793) ** 0.5
MESH = pl.DeviceIdType.MESH


def bit_axes(sizes):
    digits = []
    for name, size in sizes:
        weight = size // 2
        while weight:
            digits.append((name, weight))
            weight //= 2
    return digits


def halving_orders(digits):
    core = ("seq", 1)
    rest = [digit for digit in reversed(digits) if digit[0] == "seq" and digit != core]
    grp = [digit for digit in digits if digit[0] == "grp"]
    dp = [digit for digit in digits if digit[0] == "dp"]
    first = [core] if core in digits else []
    return (first + grp + dp + rest, first + dp + grp + rest)


def own_bit(digit):
    return lax.rem(lax.div(lax.axis_index(digit[0]), digit[1]), 2)


def partner(digit):
    name, weight = digit
    return {name: lax.axis_index(name) + (1 - 2 * own_bit(digit)) * weight}


def buffer_shapes(digits, rows, columns):
    return [
        (2,) * (len(digits) - 1 - stage) + (rows, columns) for stage in range(len(digits))
    ]


class Halving:
    def __init__(self, digits, order, chunks, part, sums, landed, out, send_sem, recv_sem):
        self.digits, self.order, self.chunks = digits, order, chunks
        self.levels = [part] + list(sums)
        self.landed, self.out = landed, out
        self.send_sem, self.recv_sem = send_sem, recv_sem
        self.width = part.shape[-1] // chunks
        self.places, left = [], list(digits)
        for digit in order:
            self.places.append(left.index(digit))
            left.remove(digit)

    def where(self, stage, chunk, bit):
        ahead = self.places[stage]
        behind = len(self.digits) - stage - 1 - ahead
        columns = pl.ds(chunk * self.width, self.width)
        index = (slice(None),) * ahead
        index += () if bit is None else (bit,)
        return index + (slice(None),) * (behind + 1) + (columns,)

    def copy(self, stage, chunk):
        digit = self.order[stage]
        return pltpu.make_async_remote_copy(
            src_ref=self.levels[stage].at[self.where(stage, chunk, 1 - own_bit(digit))],
            dst_ref=self.landed[stage].at[self.where(stage, chunk, None)],
            send_sem=self.send_sem.at[stage, chunk],
            recv_sem=self.recv_sem.at[stage, chunk],
            device_id=partner(digit),
            device_id_type=MESH,
        )

    def start(self, stage, chunk):
        self.copy(stage, chunk).start()

    def take(self, stage, chunk):
        self.copy(stage, chunk).wait_recv()
        kept = self.levels[stage][self.where(stage, chunk, own_bit(self.order[stage]))]
        place = self.where(stage, chunk, None)
        total = kept.astype(jnp.float32) + self.landed[stage][place].astype(jnp.float32)
        if stage + 1 < len(self.order):
            self.levels[stage + 1][place] = total.astype(jnp.bfloat16)
            self.start(stage + 1, chunk)
        else:
            self.out[place] = total

    def finish(self):
        for stage in range(len(self.order)):
            for chunk in range(self.chunks):
                self.copy(stage, chunk).wait_send()


EPS = 1e-06
NT = (((1,), (1,)), ((), ()))
TN = (((0,), (0,)), ((), ()))


def contract(left, right, dims):
    return lax.dot_general(left, right, dims, preferred_element_type=jnp.float32)


def aligned(start, size):
    return pl.ds(pl.multiple_of(start, size), size)


def over(count, body):
    def step(place, carry):
        body(place)
        return carry

    lax.fori_loop(0, count, step, 0)


def over_rows(array, body):
    over(array.shape[0] // ROWS, lambda place: body(aligned(place * ROWS, ROWS)))


def times(left, weight, store):
    def tile(place):
        columns = aligned(place * TILE, TILE)
        store(columns, jnp.dot(left[...], weight[:, columns], preferred_element_type=jnp.float32))

    over(weight.shape[1] // TILE, tile)


def times_back(left, weight, store):
    def tile(place):
        columns = aligned(place * TILE, TILE)
        store(columns, contract(left[...], weight[columns, :], NT))

    over(weight.shape[0] // TILE, tile)


def into(target):
    def store(columns, value):
        target[:, columns] = value.astype(target.dtype)

    return store


def unit(values):
    values = values.astype(jnp.float32)
    scale = lax.rsqrt(jnp.mean(values * values, axis=-1, keepdims=True) + EPS)
    return values * scale, scale


def unit_back(grad, units, scale):
    return scale * (grad - units * jnp.mean(grad * units, axis=-1, keepdims=True))


def norm_rows(source, gain, target):
    def block(rows):
        target[rows, :] = (unit(source[rows, :])[0] * gain[...]).astype(jnp.bfloat16)

    over_rows(source, block)


def norm_rows_back(source, gain, grad, residual, target):
    def block(rows):
        units, scale = unit(source[rows, :])
        inner = unit_back(grad[rows, :].astype(jnp.float32) * gain[...], units, scale)
        target[rows, :] = (residual[rows, :].astype(jnp.float32) + inner).astype(jnp.bfloat16)

    over_rows(source, block)


def head_parts(joined, head):
    inner = joined.shape[1] // 3
    size = inner // HEADS
    return [aligned(part * inner + head * size, size) for part in range(3)]


def head_weights(joined, columns, mask):
    queries, query_scale = unit(joined[:, columns[0]])
    keys, key_scale = unit(joined[:, columns[1]])
    query_half, key_half = queries.astype(jnp.bfloat16), keys.astype(jnp.bfloat16)
    scores = contract(query_half, key_half, NT) * queries.shape[-1] ** (-0.5)
    weights = jnp.exp(scores)
    if mask is not None:
        weights = weights * mask[...]
    weights = weights / jnp.sum(weights, axis=-1, keepdims=True)
    return weights, (queries, query_scale, query_half), (keys, key_scale, key_half)


def attend(joined, mixed):
    def head(place):
        columns = head_parts(joined, place)
        weights = head_weights(joined, columns, None)[0].astype(jnp.bfloat16)
        mixture = jnp.dot(weights, joined[:, columns[2]], preferred_element_type=jnp.float32)
        mixed[:, columns_of(mixed, place)] = mixture.astype(jnp.bfloat16)

    over(HEADS, head)


def columns_of(mixed, place):
    size = mixed.shape[1] // HEADS
    return aligned(place * size, size)


def attend_back(joined, mixed_grad, joined_grad, mask):
    def head(place):
        columns = head_parts(joined, place)
        weights, (queries, query_scale, query_half), (keys, key_scale, key_half) = head_weights(
            joined, columns, mask
        )
        grad = mixed_grad[:, columns_of(mixed_grad, place)]
        joined_grad[:, columns[2]] = contract(weights.astype(jnp.bfloat16), grad, TN).astype(
            jnp.bfloat16
        )
        weight_grad = contract(grad, joined[:, columns[2]], NT)
        weight_grad = weight_grad.astype(jnp.bfloat16).astype(jnp.float32)
        shared = jnp.sum(weights * weight_grad, axis=-1, keepdims=True)
        score_grad = weights * (weight_grad - shared) * queries.shape[-1] ** (-0.5)
        score_grad = score_grad.astype(jnp.bfloat16)
        query_grad = jnp.dot(score_grad, key_half, preferred_element_type=jnp.float32)
        key_grad = contract(score_grad, query_half, TN)
        query_grad = query_grad.astype(jnp.bfloat16).astype(jnp.float32)
        key_grad = key_grad.astype(jnp.bfloat16).astype(jnp.float32)
        joined_grad[:, columns[0]] = unit_back(query_grad, queries, query_scale).astype(
            jnp.bfloat16
        )
        joined_grad[:, columns[1]] = unit_back(key_grad, keys, key_scale).astype(jnp.bfloat16)

    over(HEADS, head)


class Exchange:
    def __init__(self, sides, source, target, send_sem, recv_sem):
        self.sides, self.source, self.target = sides, source, target
        self.send_sem, self.recv_sem = send_sem, recv_sem
        seq, scene_seqs = lax.axis_index("seq"), FRAMES // sides
        local = lax.rem(seq, scene_seqs)
        self.base = seq - local
        self.frame = local * sides + lax.axis_index("grp")
        self.size = target.shape[0] // FRAMES

    def rows(self, frame):
        return aligned(frame * self.size, self.size)

    def device(self, frame):
        return {"grp": lax.rem(frame, self.sides), "seq": self.base + lax.div(frame, self.sides)}

    def away(self, step):
        return lax.rem(self.frame + step, FRAMES)

    def copy(self, step, to, landing):
        return pltpu.make_async_remote_copy(
            src_ref=self.source.at[self.rows(to), :],
            dst_ref=self.target.at[self.rows(landing), :],
            send_sem=self.send_sem.at[step],
            recv_sem=self.recv_sem.at[step],
            device_id=self.device(to),
            device_id_type=MESH,
        )

    def start(self):
        def one(place):
            self.copy(place + 1, self.away(place + 1), self.frame).start()

        over(FRAMES - 1, one)
        own = self.rows(self.frame)
        self.target[own, :] = self.source[own, :]

    def wait(self):
        def one(place):
            step = place + 1
            sender = lax.rem(self.frame + FRAMES - step, FRAMES)
            self.copy(step, sender, sender).wait_recv()

        over(FRAMES - 1, one)

    def finish(self):
        def one(place):
            self.copy(place + 1, self.away(place + 1), self.frame).wait_send()

        over(FRAMES - 1, one)


def visible(mask, valid, sides):
    tokens = mask.shape[0] // FRAMES
    scene = lax.div(lax.axis_index("seq"), FRAMES // sides)
    limit = valid[lax.axis_index("dp"), scene]
    query = lax.broadcasted_iota(jnp.int32, mask.shape, 0)
    key = lax.broadcasted_iota(jnp.int32, mask.shape, 1)
    query_frame, key_frame = lax.div(query, tokens), lax.div(key, tokens)
    same = query - query_frame * tokens == key - key_frame * tokens
    seen = same & (key_frame <= query_frame) & (key_frame < limit)
    mask[...] = seen.astype(jnp.float32)


def weight_part(left, right, part, chunk):
    width = right.shape[1] // CHUNKS
    columns = pl.ds(chunk * width, width)
    ahead = (left.shape[1] // TILE).bit_length() - 1
    blocks = part.shape[ahead:-2]

    def tile(place):
        value = contract(left[:, aligned(place * TILE, TILE)], right[:, columns], TN)
        value = value.reshape(blocks + (part.shape[-2], width)).astype(jnp.bfloat16)
        bits = tuple(lax.rem(lax.div(place, 1 << (ahead - 1 - i)), 2) for i in range(ahead))
        part[bits + (slice(None),) * (len(blocks) + 1) + (columns,)] = value

    over(left.shape[1] // TILE, tile)


def world_kernel(
    digits,
    sides,
    valid,
    counts,
    cotangent,
    pillar_gain,
    space_gain,
    time_gain,
    *refs,
):
    weights_far, refs = refs[:7], refs[7:]
    (pillar_out, latent_out), refs = refs[:2], refs[2:]
    weights, refs = refs[:7], refs[7:]
    weight_sem, refs = refs[0], refs[1:]
    (features, before, hidden, stream, work, joined, mixed, spaced), refs = refs[:8], refs[8:]
    (tile_stream, tile_cot, joined_grad, tile_grad, back, wide, mask, tile_joined), refs = (
        refs[:8],
        refs[8:],
    )
    ways, refs = refs[:6], refs[6:]
    stages = len(digits)
    part_a, part_b = refs[:2]
    scratch = refs[2:]
    sums_a, sums_b = scratch[: stages - 1], scratch[stages - 1 : 2 * stages - 2]
    rest = scratch[2 * stages - 2 :]
    landed_a, landed_b = rest[:stages], rest[stages : 2 * stages]
    send_a, recv_a, send_b, recv_b = rest[2 * stages :]
    orders = halving_orders(digits)
    latent_sum = Halving(
        digits, orders[0], CHUNKS, part_a, sums_a, landed_a, latent_out, send_a, recv_a
    )
    pillar_sum = Halving(
        digits, orders[1], CHUNKS, part_b, sums_b, landed_b, pillar_out, send_b, recv_b
    )
    own_cot = cotangent.at[lax.axis_index("grp")]
    cot_way = Exchange(sides, own_cot, tile_cot, ways[0], ways[1])
    stream_way = Exchange(sides, spaced, tile_stream, ways[2], ways[3])
    back_way = Exchange(sides, tile_grad, back, ways[4], ways[5])

    loads = [
        pltpu.make_async_copy(far, near, weight_sem.at[place])
        for place, (far, near) in enumerate(zip(weights_far, weights))
    ]
    for load in loads:
        load.start()

    barrier = pltpu.get_barrier_semaphore()

    def greet_frame(place):
        device = cot_way.device(cot_way.away(place + 1))
        pl.semaphore_signal(barrier, inc=1, device_id=device, device_id_type=MESH)

    over(FRAMES - 1, greet_frame)
    others = [
        digit
        for digit in digits
        if digit[0] == "dp" or (digit[0] == "seq" and digit[1] >= FRAMES // sides)
    ]
    for digit in others:
        pl.semaphore_signal(barrier, inc=1, device_id=partner(digit), device_id_type=MESH)

    def features_rows(rows):
        features[rows, :] = jnp.log(1.0 + counts[rows, :].astype(jnp.float32)).astype(jnp.bfloat16)

    over_rows(features, features_rows)
    pl.semaphore_wait(barrier, FRAMES - 1 + len(others))
    cot_way.start()

    pillar_proj, latent_proj, input_proj, space_project, space_output = weights[:5]
    time_project, time_output = weights[5:]
    loads[0].wait()
    times(features, pillar_proj, into(before))

    def hidden_rows(rows):
        inputs = unit(before[rows, :])[0] * pillar_gain[...]
        bent = jnp.tanh(GELU * (inputs + 0.044715 * inputs * inputs * inputs))
        hidden[rows, :] = (0.5 * inputs * (1.0 + bent)).astype(jnp.bfloat16)

    over_rows(hidden, hidden_rows)
    loads[1].wait()
    times(hidden, latent_proj, into(work))
    loads[2].wait()
    times(work, input_proj, into(stream))
    norm_rows(stream, space_gain, work)
    loads[3].wait()
    times(work, space_project, into(joined))
    attend(joined, mixed)
    loads[4].wait()

    def space_store(columns, value):
        spaced[:, columns] = (stream[:, columns].astype(jnp.float32) + value).astype(jnp.bfloat16)

    times(mixed, space_output, space_store)
    stream_way.start()

    visible(mask, valid, sides)
    cot_way.wait()
    loads[5].wait()
    loads[6].wait()
    times_back(tile_cot, time_output, into(mixed))
    stream_way.wait()
    norm_rows(tile_stream, time_gain, work)
    times(work, time_project, into(tile_joined))
    attend_back(tile_joined, mixed, joined_grad, mask)
    times_back(joined_grad, time_project, into(work))
    norm_rows_back(tile_stream, time_gain, work, tile_cot, tile_grad)
    back_way.start()

    back_way.wait()
    times_back(back, space_output, into(mixed))
    attend_back(joined, mixed, joined_grad, None)
    times_back(joined_grad, space_project, into(work))
    norm_rows_back(stream, space_gain, work, back, mixed)
    times_back(mixed, input_proj, into(work))
    for chunk in range(CHUNKS):
        weight_part(hidden, work, part_a, chunk)
        latent_sum.start(0, chunk)
    times_back(work, latent_proj, into(wide))

    def before_rows(rows):
        units, scale = unit(before[rows, :])
        inputs = units * pillar_gain[...]
        square = inputs * inputs
        bent = jnp.tanh(GELU * (inputs + 0.044715 * square * inputs))
        slope = 0.5 * (1.0 + bent) + 0.5 * inputs * (1.0 - bent * bent) * GELU * (
            1.0 + 3 * 0.044715 * square
        )
        grad = wide[rows, :] * slope * pillar_gain[...]
        mixed[rows, :] = unit_back(grad, units, scale).astype(jnp.bfloat16)

    over_rows(before, before_rows)
    for chunk in range(CHUNKS):
        weight_part(features, mixed, part_b, chunk)
        pillar_sum.start(0, chunk)
    for stage in range(stages):
        for chunk in range(CHUNKS):
            latent_sum.take(stage, chunk)
            pillar_sum.take(stage, chunk)
    for way in (cot_way, stream_way, back_way):
        way.finish()
    latent_sum.finish()
    pillar_sum.finish()


def shards(
    sizes,
    counts,
    valid_frames,
    cotangent,
    pillar_proj,
    pillar_gain,
    latent_proj,
    input_proj,
    space_gain,
    space_project,
    space_output,
    time_gain,
    time_project,
    time_output,
):
    digits = bit_axes(sizes)
    tokens, width = counts.shape[-2:]
    model = input_proj.shape[1]
    rows = pillar_proj.shape[0] >> len(digits)
    weights = (
        pillar_proj,
        latent_proj,
        input_proj,
        space_project,
        space_output,
        time_project,
        time_output,
    )

    def half(*shape):
        return pltpu.VMEM(shape, jnp.bfloat16)

    def full(*shape):
        return pltpu.VMEM(shape, jnp.float32)

    hidden_width, latent_width = latent_proj.shape
    joined_width = space_project.shape[1]
    shapes = buffer_shapes(digits, rows, latent_width)
    shaped = (2,) * len(digits) + (rows, latent_width)
    scratch = [half(*weight.shape) for weight in weights]
    scratch += [pltpu.SemaphoreType.DMA((len(weights),))]
    scratch += [
        half(tokens, width),
        full(tokens, hidden_width),
        half(tokens, hidden_width),
        half(tokens, model),
        half(tokens, model),
        half(tokens, joined_width),
        half(tokens, model),
        half(tokens, model),
        half(tokens, model),
        half(tokens, model),
        half(tokens, joined_width),
        half(tokens, model),
        half(tokens, model),
        full(tokens, hidden_width),
        full(tokens, tokens),
        half(tokens, joined_width),
    ]
    scratch += [pltpu.SemaphoreType.DMA((FRAMES,))] * 6
    scratch += [half(*shaped)] * 2
    scratch += [half(*shape) for shape in shapes[:-1]] * 2
    scratch += [half(*shape) for shape in shapes] * 2
    scratch += [pltpu.SemaphoreType.DMA((len(digits), CHUNKS))] * 4
    vmem = pl.BlockSpec(memory_space=pltpu.VMEM)
    far = pl.BlockSpec(memory_space=pl.ANY)
    return pl.pallas_call(
        functools.partial(world_kernel, digits, dict(sizes)["grp"]),
        out_shape=[
            jax.ShapeDtypeStruct((rows, hidden_width), jnp.float32),
            jax.ShapeDtypeStruct((rows, latent_width), jnp.float32),
        ],
        in_specs=[pl.BlockSpec(memory_space=pltpu.SMEM)] + [vmem] * 5 + [far] * len(weights),
        out_specs=[vmem] * 2,
        scratch_shapes=scratch,
        compiler_params=pltpu.CompilerParams(
            collective_id=0, has_side_effects=True, vmem_limit_bytes=58 << 20
        ),
    )(
        valid_frames,
        counts.reshape(tokens, width),
        cotangent.reshape(cotangent.shape[1:]),
        pillar_gain.reshape(1, -1),
        space_gain.reshape(1, -1),
        time_gain.reshape(1, -1),
        *weights,
    )


def solution(mesh):
    placed = (
        P("dp", "seq", "grp", None, None),
        P(),
        P("dp", "seq", None, None),
        P(),
        P(),
        P(),
        P(),
        P(),
        P(),
        P(),
        P(),
        P(),
        P(),
    )
    sizes = tuple((name, mesh.shape[name]) for name in ("grp", "seq", "dp"))
    return jax.shard_map(
        functools.partial(shards, sizes),
        mesh=mesh,
        in_specs=placed,
        out_specs=(P(("grp", "seq", "dp"), None), P(("grp", "seq", "dp"), None)),
        check_vma=False,
    )
```

profile of v0, /device:TPU:0, one launch (start us, length us, event | category | flops | bytes accessed | tf_op | source)
XLA Modules:
  0.0 125.3 jit_solution(1242036727910579306)
XLA Ops:
  0.6 1.3 %copy.15.valid = s32[2,1]{1,0:T(2,128)} copy(s32[2,1]{0,1:T(1,128)} %param.14) | data formatting | bytes 16 | tf_op args[1]
  1.9 120.3 %shard_map.140 = (f32[32,1024]{1,0:T(8,128)}, f32[32,1024]{1,0:T(8,128)}) custom-call(s32[2,1]{1,0:T(2,128)} %copy.15.valid, s32[256,1024]{1,0:T(8,128)} %bitcast.5, bf16[2,256,1024]{2,1,0:T(8,128)(2,1)} %bitcast.6, f32[1,1024]{1,0:T(1,128)} %bitcast.7, f32[1,1024]{1,0:T(1,128)} %bitcast.8, f32[1,1024]{1,0:T(1,128)} %bitcast.9, bf16[1024,1024]{1,0:T(8,128)(2,1)} %refs_0_.1, ...), custom_call_target="tpu_custom_call" | custom-call | tf_op jit(solution)/shard_map/pallas_call | solution.py:529
  122.2 1.6 %copy.18 = f32[32,1024]{1,0:T(8,128)} copy(f32[32,1024]{1,0:T(8,128)} %get-tuple-element.4) | data formatting | bytes 262144
  123.8 1.6 %copy.19 = f32[32,1024]{1,0:T(8,128)} copy(f32[32,1024]{1,0:T(8,128)} %get-tuple-element.5) | data formatting | bytes 262144
where the time goes:
time: 126 us; the launch traced here: 125 us
  Pallas kernels  120 us (95%)
  local copies, waits for them, and re-layouts  4.43 us (4%)
    pallas_call x1, Pallas kernels, shards(): pl.pallas_call(functools.partial(world_kernel, digits, dict(sizes)['grp']...  120 us
    unnamed x3, local copies, waits for them, and re-layouts  4.43 us

commit v1 on v0

--- a/solution.py
+++ b/solution.py
@@ -114,12 +114,13 @@
     return pl.ds(pl.multiple_of(start, size), size)
 
 
-def over(count, body):
+def over(count, body, group=1):
     def step(place, carry):
-        body(place)
+        for member in range(group):
+            body(place * group + member)
         return carry
 
-    lax.fori_loop(0, count, step, 0)
+    lax.fori_loop(0, count // group, step, 0)
 
 
 def over_rows(array, body):
@@ -131,7 +132,7 @@
         columns = aligned(place * TILE, TILE)
         store(columns, jnp.dot(left[...], weight[:, columns], preferred_element_type=jnp.float32))
 
-    over(weight.shape[1] // TILE, tile)
+    over(weight.shape[1] // TILE, tile, 4)
 
 
 def times_back(left, weight, store):
@@ -139,7 +140,7 @@
         columns = aligned(place * TILE, TILE)
         store(columns, contract(left[...], weight[columns, :], NT))
 
-    over(weight.shape[0] // TILE, tile)
+    over(weight.shape[0] // TILE, tile, 4)
 
 
 def into(target):
@@ -189,7 +190,7 @@
     weights = jnp.exp(scores)
     if mask is not None:
         weights = weights * mask[...]
-    weights = weights / jnp.sum(weights, axis=-1, keepdims=True)
+    weights = weights * (1.0 / jnp.sum(weights, axis=-1, keepdims=True))
     return weights, (queries, query_scale, query_half), (keys, key_scale, key_half)
 
 
@@ -200,7 +201,7 @@
         mixture = jnp.dot(weights, joined[:, columns[2]], preferred_element_type=jnp.float32)
         mixed[:, columns_of(mixed, place)] = mixture.astype(jnp.bfloat16)
 
-    over(HEADS, head)
+    over(HEADS, head, 2)
 
 
 def columns_of(mixed, place):
@@ -232,7 +233,7 @@
         )
         joined_grad[:, columns[1]] = unit_back(key_grad, keys, key_scale).astype(jnp.bfloat16)
 
-    over(HEADS, head)
+    over(HEADS, head, 2)
 
 
 class Exchange:

time: 126 us -> 112 us (0.89)
  Pallas kernels: 120 us -> 107 us
    pallas_call x1, Pallas kernels: 120 us -> 107 us  [shards(): pl.pallas_call(functools.partial(world_kernel, digits, dict(sizes)['grp']...]
where the time goes in v1:
time: 112 us
  Pallas kernels  107 us (96%)
  local copies, waits for them, and re-layouts  4.43 us (4%)
    pallas_call x1, Pallas kernels, shards(): pl.pallas_call(functools.partial(world_kernel, digits, dict(sizes)['grp']...  107 us
    unnamed x3, local copies, waits for them, and re-layouts  4.43 us

profile of v1, /device:TPU:0, one launch (start us, length us, event | category | flops | bytes accessed | tf_op | source)
XLA Modules:
  0.0 112.2 jit_solution(5105414929356253829)
XLA Ops:
  0.6 1.3 %copy.15.valid = s32[2,1]{1,0:T(2,128)} copy(s32[2,1]{0,1:T(1,128)} %param.14) | data formatting | bytes 16 | tf_op args[1]
  1.9 107.1 %shard_map.140 = (f32[32,1024]{1,0:T(8,128)}, f32[32,1024]{1,0:T(8,128)}) custom-call(s32[2,1]{1,0:T(2,128)} %copy.15.valid, s32[256,1024]{1,0:T(8,128)} %bitcast.5, bf16[2,256,1024]{2,1,0:T(8,128)(2,1)} %bitcast.6, f32[1,1024]{1,0:T(1,128)} %bitcast.7, f32[1,1024]{1,0:T(1,128)} %bitcast.8, f32[1,1024]{1,0:T(1,128)} %bitcast.9, bf16[1024,1024]{1,0:T(8,128)(2,1)} %refs_0_.1, ...), custom_call_target="tpu_custom_call" | custom-call | tf_op jit(solution)/shard_map/pallas_call | solution.py:530
  109.1 1.6 %copy.18 = f32[32,1024]{1,0:T(8,128)} copy(f32[32,1024]{1,0:T(8,128)} %get-tuple-element.4) | data formatting | bytes 262144
  110.6 1.6 %copy.19 = f32[32,1024]{1,0:T(8,128)} copy(f32[32,1024]{1,0:T(8,128)} %get-tuple-element.5) | data formatting | bytes 262144
